TPU v7x, 128 devices: a whole 4x4x4 slice. The times are simulated.
128 devices in a mesh: pipe: 4 (over y), dp: 16 (over x, z), tensor: 2 (over core).
Axes of the slice: x: 4, y: 4, z: 4, core: 2. Of those that a mesh axis runs over, the one named last changes fastest.
Arguments:
- inputs: bfloat16 [4, 512, 4096], P(None, 'dp', 'tensor'), may hold values from -6 to 6
- weights: bfloat16 [4, 4096, 4096], P('pipe', None, 'tensor'), may hold values from -0.09375 to 0.09375
- norm_gains: float32 [4, 4096], P('pipe'), may hold values from 0.5 to 2
- cotangent: bfloat16 [4, 512, 4096], P(None, 'dp', 'tensor'), may hold values from -0.625 to 0.625
- owner_table: int32 [4, 2, 32], P('pipe', 'tensor'), may hold values from 0 to 31, each once within a row
- left_roots: float32 [4, 2, 32, 512, 512], P('pipe', 'tensor', 'dp'), may hold values from -3 to 5, as said below
- right_roots: float32 [4, 2, 32, 512, 512], P('pipe', 'tensor', 'dp'), may hold values from -3 to 5, as said below
Outputs:
- precond_update: bfloat16 [4, 4096, 4096], P('pipe', 'dp', 'tensor')
Inputs may be any that keep to these rules, and one draw needn't show every extreme that they name: `owner_table`: for each section and part, every slot number appears once; slot q lives on dp index q // 2. `left_roots`: symmetric matrices. `right_roots`: symmetric matrices.
All inputs are finite; a program needn't handle non-finite values.
Results may differ from a plain program's by a relative error of at most 0.025.
Values may be sent and summed in bfloat16 or wider, within the bound.
A program may use at most 192 MiB of HBM per device.

v0:
```python
import jax
import jax.numpy as jnp
from jax import lax
from jax.sharding import PartitionSpec as P

norm_eps = 1e-05
highest = lax.Precision.HIGHEST


def shifted(value, axis, steps):
    count = lax.axis_size(axis)
    initial, last = (max(0, -steps), min(count, count - steps))
    return lax.ppermute(value, axis, [(source, source + steps) for source in range(initial, last)])


def silu_slope(pre_act):
    logistic = jax.nn.sigmoid(pre_act)
    return logistic * (1.0 + pre_act * (1.0 - logistic))


def keep_entry(stack, value, index, active):
    former = lax.dynamic_index_in_dim(stack, index, 0, keepdims=False)
    return lax.dynamic_update_index_in_dim(stack, jnp.where(active, value, former), index, 0)


def on_device(inputs, weights, norm_gains, cotangent, owner_table, left_roots, right_roots):
    sections = lax.axis_size("pipe")
    section_pos = lax.axis_index("pipe")
    dp_count = lax.axis_size("dp")
    dp_pos = lax.axis_index("dp")
    half_pos = lax.axis_index("tensor")
    weight = weights[0]
    width = weight.shape[0]
    half_width = weight.shape[1]
    micro = inputs.shape[0]
    tok_rows = inputs.shape[1]
    gain = norm_gains[0]
    order = owner_table[0, 0]
    left_own = left_roots[0, 0]
    right_own = right_roots[0, 0]
    slots = left_own.shape[0]
    block = left_own.shape[1]
    col_blocks = half_width // block
    group_blocks = order.shape[0]
    slab_rows = width // dp_count
    piece_rows = min(slab_rows, block)
    my_start = dp_pos * slab_rows
    numbers = jnp.arange(group_blocks, dtype=jnp.int32)
    block_at_slot = jnp.sum(
        numbers[None, :] * (order[None, :] == numbers[:, None]).astype(jnp.int32), axis=1
    )
    full_store = jnp.zeros((micro, tok_rows, width), jnp.bfloat16)
    norm_store = jnp.zeros((micro, tok_rows, width), jnp.bfloat16)
    pre_store = jnp.zeros((micro, tok_rows, half_width), jnp.float32)
    scale_store = jnp.zeros((micro, tok_rows, 1), jnp.float32)
    outgoing = jnp.zeros((tok_rows, half_width), jnp.bfloat16)
    for moment in range(micro + sections - 1):
        incoming = shifted(outgoing, "pipe", 1)
        batch_idx = moment - section_pos
        active = (batch_idx >= 0) & (batch_idx < micro)
        slot_batch = jnp.clip(batch_idx, 0, micro - 1)
        half_states = jnp.where(section_pos == 0, inputs[min(moment, micro - 1)], incoming)
        full_states = lax.all_gather(half_states, "tensor", axis=1, tiled=True)
        states_f = full_states.astype(jnp.float32)
        inv_rms = lax.rsqrt(jnp.mean(states_f * states_f, axis=1, keepdims=True) + norm_eps)
        normed = (states_f * inv_rms * gain).astype(jnp.bfloat16)
        pre_act = jnp.dot(normed, weight, preferred_element_type=jnp.float32)
        outgoing = (half_states.astype(jnp.float32) + jax.nn.silu(pre_act)).astype(jnp.bfloat16)
        full_store = keep_entry(full_store, full_states, slot_batch, active)
        norm_store = keep_entry(norm_store, normed, slot_batch, active)
        pre_store = keep_entry(pre_store, pre_act, slot_batch, active)
        scale_store = keep_entry(scale_store, inv_rms, slot_batch, active)
    grad_store = jnp.zeros((micro, tok_rows, half_width), jnp.bfloat16)
    outgoing = jnp.zeros((tok_rows, half_width), jnp.bfloat16)
    for moment in range(micro + sections - 1):
        incoming = shifted(outgoing, "pipe", -1)
        batch_idx = moment - (sections - 1 - section_pos)
        active = (batch_idx >= 0) & (batch_idx < micro)
        slot_batch = jnp.clip(batch_idx, 0, micro - 1)
        grad_half = jnp.where(
            section_pos == sections - 1, cotangent[min(moment, micro - 1)], incoming
        )
        full_states = lax.dynamic_index_in_dim(full_store, slot_batch, 0, keepdims=False)
        pre_act = lax.dynamic_index_in_dim(pre_store, slot_batch, 0, keepdims=False)
        inv_rms = lax.dynamic_index_in_dim(scale_store, slot_batch, 0, keepdims=False)
        grad_f = grad_half.astype(jnp.float32)
        dpre = (grad_f * silu_slope(pre_act)).astype(jnp.bfloat16)
        dnorm_part = lax.dot_general(
            dpre, weight, (((1,), (1,)), ((), ())), preferred_element_type=jnp.float32
        )
        states_f = full_states.astype(jnp.float32)
        states_half = lax.dynamic_slice_in_dim(states_f, half_pos * half_width, half_width, 1)
        dnormed = lax.psum(dnorm_part.astype(jnp.bfloat16), "tensor").astype(jnp.float32)
        upstream = dnormed * gain
        statistic = jnp.sum(upstream * states_f * inv_rms, axis=1, keepdims=True)
        up_half = lax.dynamic_slice_in_dim(upstream, half_pos * half_width, half_width, 1)
        dstates = inv_rms * (up_half - states_half * inv_rms * statistic / width)
        outgoing = (grad_f + dstates).astype(jnp.bfloat16)
        grad_store = keep_entry(grad_store, dpre, slot_batch, active)
    norm_flat = norm_store.reshape(micro * tok_rows, width)
    grad_flat = grad_store.reshape(micro * tok_rows, half_width)
    weight_grad = lax.dot_general(
        norm_flat, grad_flat, (((0,), (0,)), ((), ())), preferred_element_type=jnp.float32
    )
    grad_term = weight_grad.astype(jnp.bfloat16)
    slab = (
        lax.psum_scatter(grad_term, "dp", scatter_dimension=0, tiled=True)
        .astype(jnp.float32)
        .astype(jnp.bfloat16)
    )

    def cut_piece(flat_slot):
        blk_num = block_at_slot[flat_slot]
        band = blk_num // col_blocks
        column = blk_num % col_blocks
        inside = (my_start < band * block + block) & (band * block < my_start + slab_rows)
        offset = jnp.maximum(band * block - my_start, 0)
        piece = lax.dynamic_slice(slab, (offset, column * block), (piece_rows, block))
        return jnp.where(inside, piece, jnp.zeros_like(piece))

    sending = jax.vmap(cut_piece)(jnp.arange(dp_count * slots, dtype=jnp.int32))
    sending = sending.reshape(dp_count, slots, piece_rows, block)
    arrived = lax.all_to_all(sending, "dp", split_axis=0, concat_axis=0, tiled=True)
    sources = block // piece_rows

    def assemble(slot_pos):
        blk_num = block_at_slot[dp_pos * slots + slot_pos]
        first_source = blk_num // col_blocks * block // slab_rows
        part_rows = lax.dynamic_slice(
            arrived, (first_source, slot_pos, 0, 0), (sources, 1, piece_rows, block)
        )
        return part_rows.reshape(block, block)

    owned = jax.vmap(assemble)(jnp.arange(slots, dtype=jnp.int32)).astype(jnp.float32)
    lefted = jnp.einsum("sij,sjk->sik", left_own, owned, precision=highest)
    result = jnp.einsum("sij,sjk->sik", lefted, right_own, precision=highest).astype(jnp.bfloat16)

    def give_piece(flat_slot):
        target = flat_slot // slots
        slot_pos = flat_slot % slots
        blk_num = block_at_slot[dp_pos * slots + slot_pos]
        band = blk_num // col_blocks
        inside = (target * slab_rows < band * block + block) & (
            band * block < target * slab_rows + slab_rows
        )
        offset = jnp.maximum(target * slab_rows - band * block, 0)
        piece = lax.dynamic_slice(result, (slot_pos, offset, 0), (1, piece_rows, block))[0]
        return jnp.where(inside, piece, jnp.zeros_like(piece))

    giving = jax.vmap(give_piece)(jnp.arange(dp_count * slots, dtype=jnp.int32))
    giving = giving.reshape(dp_count, slots, piece_rows, block)
    returned = lax.all_to_all(giving, "dp", split_axis=0, concat_axis=0, tiled=True)
    returned = returned.reshape(dp_count * slots, piece_rows, block)
    my_bands = slab_rows // piece_rows
    first_band = my_start // block
    wanted = (first_band + jnp.arange(my_bands, dtype=jnp.int32))[
        :, None
    ] * col_blocks + jnp.arange(col_blocks, dtype=jnp.int32)[None, :]
    picked = jnp.take(returned, order[wanted.reshape(-1)], axis=0)
    picked = picked.reshape(my_bands, col_blocks, piece_rows, block).transpose(0, 2, 1, 3)
    return picked.reshape(slab_rows, half_width)[None]


def solution(mesh):
    return jax.shard_map(
        on_device,
        mesh=mesh,
        in_specs=(
            P(None, "dp", "tensor"),
            P("pipe", None, "tensor"),
            P("pipe", None),
            P(None, "dp", "tensor"),
            P("pipe", "tensor", None),
            P("pipe", "tensor", "dp", None, None),
            P("pipe", "tensor", "dp", None, None),
        ),
        out_specs=P("pipe", "dp", "tensor"),
        check_vma=False,
    )
```

profile of v0, /device:TPU:100, one launch (start us, length us, event | category | flops | bytes accessed | tf_op | source)
XLA Modules:
  0.0 1046.5 jit_solution(5315970745536870054)
XLA Ops:
  7.2 3.6 collective-permute-start
  17.0 9.0 add_convert_fusion.5
  26.0 4.3 collective-permute-start.1
  35.6 3.1 add_convert_fusion.4
  38.8 4.4 collective-permute-start.2
  43.5 2.7 collective-permute-done.2
  48.4 3.1 add_convert_fusion.3
  51.5 4.4 collective-permute-start.3
  56.3 2.7 collective-permute-done.3
  61.4 3.1 add_convert_fusion.2
  64.5 4.4 collective-permute-start.4
  69.2 2.7 collective-permute-done.4
  74.1 3.1 add_convert_fusion.1
  77.2 4.4 collective-permute-start.5
  82.0 2.7 collective-permute-done.5
  86.9 3.1 add_convert_fusion
  90.0 4.4 collective-permute-start.6
  99.9 3.1 fusion.50
  105.9 11.6 %fusion.26 = bf16[32,4096]{1,0:T(8,128)(2,1)} fusion(bf16[32,2048]{1,0:T(8,128)(2,1)S(1)} %get-tuple-element.48, bf16[1,4096,2048]{2,1,0:T(8,128)(2,1)} %param.8), kind=kOutput, calls=%fused_computation.39 | convolution fusion | flops 537001984 | bytes 17170432 | tf_op jit(solution)/shard_map/dot_general | solution.py:88
  123.7 20.0 %all-reduce.7.cloned.1.call-done = bf16[32,4096]{1,0:T(8,128)(2,1)} async-done(((bf16[32,4096]{1,0:T(8,128)(2,1)}), bf16[32,4096]{1,0:T(8,128)(2,1)}) %all-reduce.7.cloned.1.call-update) | async-done | bytes 262160 | tf_op jit(solution)/shard_map/psum | solution.py:93
  148.7 4.9 collective-permute-done.8
  155.4 11.6 %fusion.29 = bf16[32,4096]{1,0:T(8,128)(2,1)} fusion(bf16[32,2048]{1,0:T(8,128)(2,1)S(1)} %get-tuple-element.46, bf16[1,4096,2048]{2,1,0:T(8,128)(2,1)} %param.8), kind=kOutput, calls=%fused_computation.40 | convolution fusion | flops 537001984 | bytes 17170432 | tf_op jit(solution)/shard_map/dot_general | solution.py:88
  167.0 25.3 %all-reduce.9.cloned.1.call-done = bf16[32,4096]{1,0:T(8,128)(2,1)} async-done(((bf16[32,4096]{1,0:T(8,128)(2,1)}), bf16[32,4096]{1,0:T(8,128)(2,1)}) %all-reduce.9.cloned.1.call-update) | async-done | bytes 262160 | tf_op jit(solution)/shard_map/psum | solution.py:93
  196.8 5.4 collective-permute-done.9
  203.9 11.6 %fusion.32 = bf16[32,4096]{1,0:T(8,128)(2,1)} fusion(bf16[32,2048]{1,0:T(8,128)(2,1)S(1)} %get-tuple-element.44, bf16[1,4096,2048]{2,1,0:T(8,128)(2,1)} %param.8), kind=kOutput, calls=%fused_computation.41 | convolution fusion | flops 537001984 | bytes 17170432 | tf_op jit(solution)/shard_map/dot_general | solution.py:88
  215.6 25.3 %all-reduce.11.cloned.1.call-done = bf16[32,4096]{1,0:T(8,128)(2,1)} async-done(((bf16[32,4096]{1,0:T(8,128)(2,1)}), bf16[32,4096]{1,0:T(8,128)(2,1)}) %all-reduce.11.cloned.1.call-update) | async-done | bytes 262160 | tf_op jit(solution)/shard_map/psum | solution.py:93
  245.5 5.2 collective-permute-done.10
  252.5 11.6 %fusion.35 = bf16[32,4096]{1,0:T(8,128)(2,1)} fusion(bf16[32,2048]{1,0:T(8,128)(2,1)S(1)} %get-tuple-element.42, bf16[1,4096,2048]{2,1,0:T(8,128)(2,1)} %param.8), kind=kOutput, calls=%fused_computation.42 | convolution fusion | flops 537001984 | bytes 17170432 | tf_op jit(solution)/shard_map/dot_general | solution.py:88
  264.2 25.3 %all-reduce.13.cloned.1.call-done = bf16[32,4096]{1,0:T(8,128)(2,1)} async-done(((bf16[32,4096]{1,0:T(8,128)(2,1)}), bf16[32,4096]{1,0:T(8,128)(2,1)}) %all-reduce.13.cloned.1.call-update) | async-done | bytes 262160 | tf_op jit(solution)/shard_map/psum | solution.py:93
  293.9 5.4 collective-permute-done.11
  301.1 11.6 %fusion.38 = bf16[32,4096]{1,0:T(8,128)(2,1)} fusion(bf16[32,2048]{1,0:T(8,128)(2,1)S(1)} %get-tuple-element.40, bf16[1,4096,2048]{2,1,0:T(8,128)(2,1)} %param.8), kind=kOutput, calls=%fused_computation.43 | convolution fusion | flops 537001984 | bytes 17170432 | tf_op jit(solution)/shard_map/dot_general | solution.py:88
  312.8 25.3 %all-reduce.15.cloned.1.call-done = bf16[32,4096]{1,0:T(8,128)(2,1)} async-done(((bf16[32,4096]{1,0:T(8,128)(2,1)}), bf16[32,4096]{1,0:T(8,128)(2,1)}) %all-reduce.15.cloned.1.call-update) | async-done | bytes 262160 | tf_op jit(solution)/shard_map/psum | solution.py:93
  342.8 5.2 collective-permute-done.12
  349.7 11.6 %fusion.41 = bf16[32,4096]{1,0:T(8,128)(2,1)} fusion(bf16[32,2048]{1,0:T(8,128)(2,1)S(1)} %get-tuple-element.38, bf16[1,4096,2048]{2,1,0:T(8,128)(2,1)} %param.8), kind=kOutput, calls=%fused_computation.44 | convolution fusion | flops 537001984 | bytes 17170432 | tf_op jit(solution)/shard_map/dot_general | solution.py:88
  361.3 25.3 %all-reduce.17.cloned.1.call-done = bf16[32,4096]{1,0:T(8,128)(2,1)} async-done(((bf16[32,4096]{1,0:T(8,128)(2,1)}), bf16[32,4096]{1,0:T(8,128)(2,1)}) %all-reduce.17.cloned.1.call-update) | async-done | bytes 262160 | tf_op jit(solution)/shard_map/psum | solution.py:93
  391.1 5.4 collective-permute-done.13
  398.3 11.6 %bitcast_convert_fusion = bf16[4096,2048]{1,0:T(8,128)(2,1)} fusion(bf16[4,32,4096]{2,1,0:T(8,128)(2,1)} %get-tuple-element.70, bf16[4,32,2048]{2,1,0:T(8,128)(2,1)} %bitcast_dynamic-update-slice_fusion.22), kind=kOutput, calls=%fused_computation.10 | convolution fusion | flops 2155872256 | bytes 18350080 | tf_op jit(solution)/shard_map/dot_general | solution.py:102
  412.4 107.7 %reduce-scatter.2.cloned.1.call-done = bf16[256,2048]{1,0:T(8,128)(2,1)} async-done(((bf16[4096,2048]{1,0:T(8,128)(2,1)}), bf16[256,2048]{1,0:T(8,128)(2,1)}) %reduce-scatter.2.cloned.1.call-update) | async-done | bytes 1048592 | tf_op jit(solution)/shard_map/reduce_scatter | solution.py:107
  520.1 101.9 %while.2 = (s32[]{:T(128)}, bf16[256,2048]{1,0:T(8,128)(2,1)}, s32[32,2]{0,1:T(2,128)S(1)}, bf16[32,256,512]{2,1,0:T(8,128)(2,1)}, s32[]{:T(128)}) while((s32[]{:T(128)}, bf16[256,2048]{1,0:T(8,128)(2,1)}, s32[32,2]{0,1:T(2,128)S(1)}, bf16[32,256,512]{2,1,0:T(8,128)(2,1)}, s32[]{:T(128)}) %tuple.68), condition=%wide.while_cond, body=%wide.while_body.sunk | while | flops 2 | bytes 525401 | solution.py:118
  520.8 2.5 bitcast_dynamic-update-slice_fusion.31
  524.0 2.5 bitcast_dynamic-update-slice_fusion.31
  533.5 2.5 bitcast_dynamic-update-slice_fusion.31
  539.9 2.5 bitcast_dynamic-update-slice_fusion.31
  546.3 2.5 bitcast_dynamic-update-slice_fusion.31
  549.5 2.5 bitcast_dynamic-update-slice_fusion.31
  562.2 2.5 bitcast_dynamic-update-slice_fusion.31
  574.9 2.5 bitcast_dynamic-update-slice_fusion.31
  578.1 2.5 bitcast_dynamic-update-slice_fusion.31
  581.3 2.5 bitcast_dynamic-update-slice_fusion.31
  587.6 2.5 bitcast_dynamic-update-slice_fusion.31
  590.8 2.5 bitcast_dynamic-update-slice_fusion.31
  597.2 2.5 bitcast_dynamic-update-slice_fusion.31
  600.4 2.5 bitcast_dynamic-update-slice_fusion.31
  613.1 2.5 bitcast_dynamic-update-slice_fusion.31
  622.0 7.3 broadcast_select_fusion
  629.3 7.7 all-to-all-start
  637.7 148.4 %all-to-all-done = bf16[16,2,256,512]{3,2,1,0:T(8,128)(2,1)} async-done(((bf16[16,2,256,512]{3,2,1,0:T(8,128)(2,1)}), bf16[16,2,256,512]{3,2,1,0:T(8,128)(2,1)}, u32[]{:S(2)}, u32[]{:S(2)}) %all-to-all-start) | async-done | bytes 8388640 | tf_op jit(solution)/shard_map/all_to_all | solution.py:123
  786.1 4.0 gather_fusion.4
  792.0 5.1 fusion.57
  797.1 86.7 %while.3 = (s32[]{:T(128)}, bf16[2,512,512]{2,1,0:T(8,128)(2,1)S(1)}, s32[32,3]{0,1:T(4,128)S(1)}, bf16[32,1,256,512]{3,2,1,0:T(8,128)(2,1)}, s32[]{:T(128)}) while((s32[]{:T(128)}, bf16[2,512,512]{2,1,0:T(8,128)(2,1)S(1)}, s32[32,3]{0,1:T(4,128)S(1)}, bf16[32,1,256,512]{3,2,1,0:T(8,128)(2,1)}, s32[]{:T(128)}) %tuple.71), condition=%wide.while_cond.1, body=%wide.while_body.1.sunk | while | flops 2 | bytes 525929 | solution.py:147
  883.8 7.3 bitcast_select_fusion
  891.1 6.9 all-to-all-start.1
  898.7 135.3 %all-to-all-done.1 = bf16[16,2,256,512]{3,2,1,0:T(8,128)(2,1)} async-done(((bf16[16,2,256,512]{3,2,1,0:T(8,128)(2,1)}), bf16[16,2,256,512]{3,2,1,0:T(8,128)(2,1)}, u32[]{:S(2)}, u32[]{:S(2)}) %all-to-all-start.1) | async-done | bytes 8388640 | tf_op jit(solution)/shard_map/all_to_all | solution.py:152
  1034.0 4.0 gather_fusion.5
  (370 shorter events, 232.9 us)
Async XLA Ops:
  6.5 783.6 %copy-start = (f32[1,1,2,512,512]{4,3,2,1,0:T(8,128)S(1)}, f32[1,1,2,512,512]{4,3,2,1,0:T(8,128)}, u32[]{:S(2)}) copy-start(f32[1,1,2,512,512]{4,3,2,1,0:T(8,128)} %param.12) | copy-start | bytes 6291460
  6.5 23.9 %copy-start.3 = (f32[1,4096]{1,0:T(1,128)S(1)}, f32[1,4096]{1,0:T(1,128)}, u32[]{:S(2)}) copy-start(f32[1,4096]{1,0:T(1,128)} %param.9) | copy-start | bytes 49156
  6.5 137.2 %all-reduce.7.cloned.1.call-start = ((), (), s32[]{:S(2)}) async-start(), calls=%async_computation.3 | async-start | bytes 524288 | tf_op jit(solution)/shard_map/psum | solution.py:93
  7.2 6.7 collective-permute-start
  10.8 92.2 %collective-permute-start.7 = (bf16[32,2048]{1,0:T(8,128)(2,1)}, bf16[32,2048]{1,0:T(8,128)(2,1)S(1)}, u32[]{:S(2)}, u32[]{:S(2)}) collective-permute-start(bf16[32,2048]{1,0:T(8,128)(2,1)} %broadcast.925), channel_id=1, source_target_pairs={{32,0},{64,32},{96,64},{33,1},{65,33},{97,65},{34,2},{66,34},{98,6... | collective-permute-start | bytes 393224 | tf_op jit(solution)/shard_map/ppermute | solution.py:13
  12.2 21.2 %copy-start.6 = (bf16[4,32,2048]{2,1,0:T(8,128)(2,1)S(1)}, bf16[4,32,2048]{2,1,0:T(8,128)(2,1)}, u32[]{:S(2)}) copy-start(bf16[4,32,2048]{2,1,0:T(8,128)(2,1)} %param.7) | copy-start | bytes 1572868
  12.2 23.4 %slice-start = ((s8[16777216]{0:T(1024)(128)(4,1)}), s8[4194304]{0:T(1024)(128)(4,1)S(1)}, s32[]{:S(2)}) async-start(s8[16777216]{0:T(1024)(128)(4,1)} %bitcast.634), calls=%async_computation.10 | async-start | bytes 8388608
  17.0 18.6 %slice-start.1 = ((s8[16777216]{0:T(1024)(128)(4,1)}), s8[4194304]{0:T(1024)(128)(4,1)S(1)}, s32[]{:S(2)}) async-start(s8[16777216]{0:T(1024)(128)(4,1)} %bitcast.634), calls=%async_computation.11 | async-start | bytes 8388608
  17.0 18.6 %slice-start.2 = ((s8[16777216]{0:T(1024)(128)(4,1)}), s8[4194304]{0:T(1024)(128)(4,1)S(1)}, s32[]{:S(2)}) async-start(s8[16777216]{0:T(1024)(128)(4,1)} %bitcast.634), calls=%async_computation.12 | async-start | bytes 8388608
  17.0 18.6 %slice-start.3 = ((s8[16777216]{0:T(1024)(128)(4,1)}), s8[4194304]{0:T(1024)(128)(4,1)S(1)}, s32[]{:S(2)}) async-start(s8[16777216]{0:T(1024)(128)(4,1)} %bitcast.634), calls=%async_computation.13 | async-start | bytes 8388608
  26.0 7.4 collective-permute-start.1
  38.8 7.4 collective-permute-start.2
  51.5 7.4 collective-permute-start.3
  64.5 7.4 collective-permute-start.4
  77.2 7.4 collective-permute-start.5
  90.0 7.4 collective-permute-start.6
  94.7 10.3 copy-start.4
  96.2 8.8 copy-start.7
  99.9 5.2 copy-start.14
  99.9 5.2 copy-start.13
  103.0 1.0 copy-start.2
  105.1 0.8 copy-start.5
  117.5 74.8 %all-reduce.9.cloned.1.call-start = ((), (), s32[]{:S(2)}) async-start(), calls=%async_computation.4 | async-start | bytes 524288 | tf_op jit(solution)/shard_map/psum | solution.py:93
  146.0 46.3 %copy-start.12 = (f32[32]{0:T(128)S(1)}, f32[32]{0:T(128)}, u32[]{:S(2)}) copy-start(f32[32]{0:T(128)} %get-tuple-element.85) | copy-start | bytes 388
  146.0 7.6 collective-permute-start.8
  155.4 85.5 %copy-start.11 = (f32[32]{0:T(128)S(1)}, f32[32]{0:T(128)}, u32[]{:S(2)}) copy-start(f32[32]{0:T(128)} %get-tuple-element.84) | copy-start | bytes 388
  167.0 73.9 %all-reduce.11.cloned.1.call-start = ((), (), s32[]{:S(2)}) async-start(), calls=%async_computation.5 | async-start | bytes 524288 | tf_op jit(solution)/shard_map/psum | solution.py:93
  194.6 7.6 collective-permute-start.9
  203.9 85.5 %copy-start.10 = (f32[32]{0:T(128)S(1)}, f32[32]{0:T(128)}, u32[]{:S(2)}) copy-start(f32[32]{0:T(128)} %get-tuple-element.83) | copy-start | bytes 388
  215.5 73.9 %all-reduce.13.cloned.1.call-start = ((), (), s32[]{:S(2)}) async-start(), calls=%async_computation.6 | async-start | bytes 524288 | tf_op jit(solution)/shard_map/psum | solution.py:93
  243.1 7.6 collective-permute-start.10
  252.5 85.5 %copy-start.9 = (f32[32]{0:T(128)S(1)}, f32[32]{0:T(128)}, u32[]{:S(2)}) copy-start(f32[32]{0:T(128)} %get-tuple-element.82) | copy-start | bytes 388
  264.1 73.9 %all-reduce.15.cloned.1.call-start = ((), (), s32[]{:S(2)}) async-start(), calls=%async_computation.7 | async-start | bytes 524288 | tf_op jit(solution)/shard_map/psum | solution.py:93
  291.7 7.6 collective-permute-start.11
  301.1 85.5 %copy-start.8 = (f32[32]{0:T(128)S(1)}, f32[32]{0:T(128)}, u32[]{:S(2)}) copy-start(f32[32]{0:T(128)} %get-tuple-element.81) | copy-start | bytes 388
  312.7 73.9 %all-reduce.17.cloned.1.call-start = ((), (), s32[]{:S(2)}) async-start(), calls=%async_computation.8 | async-start | bytes 524288 | tf_op jit(solution)/shard_map/psum | solution.py:93
  340.3 7.6 collective-permute-start.12
  361.3 158.8 %reduce-scatter.2.cloned.1.call-start = ((), (), s32[]{:S(2)}) async-start(), calls=%async_computation.9 | async-start | bytes 17825792 | tf_op jit(solution)/shard_map/reduce_scatter | solution.py:107
  388.9 7.6 collective-permute-start.13
  409.9 0.7 copy-start.1
  629.3 156.8 %all-to-all-start = ((bf16[16,2,256,512]{3,2,1,0:T(8,128)(2,1)}), bf16[16,2,256,512]{3,2,1,0:T(8,128)(2,1)}, u32[]{:S(2)}, u32[]{:S(2)}) async-start(bf16[16,2,256,512]{3,2,1,0:T(8,128)(2,1)} %broadcast_select_fusion), calls=%async_computation.1 | async-start | bytes 16777216 | tf_op jit(solution)/shard_map/all_to_all | solution.py:123
  891.1 142.9 %all-to-all-start.1 = ((bf16[16,2,256,512]{3,2,1,0:T(8,128)(2,1)}), bf16[16,2,256,512]{3,2,1,0:T(8,128)(2,1)}, u32[]{:S(2)}, u32[]{:S(2)}) async-start(bf16[16,2,256,512]{3,2,1,0:T(8,128)(2,1)} %bitcast_select_fusion), calls=%async_computation.2 | async-start | bytes 16777216 | tf_op jit(solution)/shard_map/all_to_all | solution.py:152
Sparse Core Ops, SparseCore 0:
  117.6 26.0 all-reduce.6
  167.1 25.1 all-reduce.8
  215.7 25.1 all-reduce.10
  264.2 25.1 all-reduce.12
  312.8 25.1 all-reduce.14
  361.4 25.1 all-reduce.16
  410.1 109.9 reduce-scatter.1
where the time goes:
time: 1060 us; the launch traced here: 1050 us
  waiting for transfers between devices  585 us (55%)
  local copies, waits for them, and re-layouts  213 us (20%)
  matrix products  116 us (11%)
  starting transfers between devices  54.6 us (5%)
  other arithmetic  48.9 us (5%)
  between operations  14.9 us (1%)
  blocking collectives  14.4 us (1%)
    gather x192, local copies, waits for them, and re-layouts  188 us
    all_to_all x1, waiting for transfers between devices, on_device(): lax.all_to_all(sending, 'dp', split_axis=0, concat_axis=0, tiled=True)  148 us
    psum x6, waiting for transfers between devices, on_device(): lax.psum(dnorm_part.astype(jnp.bfloat16), 'tensor').astype(jnp.float32)  146 us
    all_to_all x1, waiting for transfers between devices, on_device(): lax.all_to_all(giving, 'dp', split_axis=0, concat_axis=0, tiled=True)  135 us
    reduce_scatter x1, waiting for transfers between devices, on_device(): lax.psum_scatter(grad_term, 'dp', scatter_dimension=0, tiled=True)  108 us
    dot_general x6, matrix products, on_device(): lax.dot_general(dpre, weight, (((1,), (1,)), ((), ())), preferred_element...  69.5 us
    ppermute x14, waiting for transfers between devices, shifted(): lax.ppermute(value, axis, [(source, source + steps) for source in range(i...  47.3 us
    ppermute x14, starting transfers between devices, shifted(): lax.ppermute(value, axis, [(source, source + steps) for source in range(i...  39.8 us
  transfers between devices with their start and end apart: 23, of which 22 were waited for; matrix products, arithmetic and copies ran while one was open for 5% of the time, Pallas kernels for 0%

commit v1 on v0

v1 whole, which is shorter than its diff:
```python
import functools

import jax
import jax.numpy as jnp
from jax import lax
from jax.experimental import pallas as pl
from jax.experimental.pallas import tpu as pltpu
from jax.sharding import PartitionSpec as P

MESH = pl.DeviceIdType.MESH
norm_eps = 1e-05
GROUPS = ((0, 48), (48, 48), (96, 32))
N_GROUPS = len(GROUPS)
CHUNK = 512
N_CHUNKS = 4
DIRECT = (N_GROUPS - 1,)


def remote(src, dst, send, recv, target):
    return pltpu.make_async_remote_copy(
        src_ref=src, dst_ref=dst, send_sem=send, recv_sem=recv, device_id=target, device_id_type=MESH
    )


def each(low, high, body):
    def step(index, carry):
        body(index)
        return carry

    lax.fori_loop(low, high, step, 0)


def plan_of(section):
    groups = range(N_GROUPS)

    def every(kind):
        return [kind + str(i) for i in groups]

    plan = ["R1"] + ["T"] * (section >= 2)
    if section == 3:
        for i in groups:
            plan += ["F%d" % i, "B%d" % i]
            plan += ["R2"] * (i == 0)
            plan += ["X%d" % i]
        for i in groups:
            plan += ["d%d" % i, "n%d" % i]
        plan += ["N", "U"] + every("G")
    else:
        for i in groups:
            plan += ["F%d" % i, "X%d" % i]
        if section == 0:
            plan += every("n") + ["R2", "N", "U"]
            for i in groups:
                plan += ["B%d" % i]
                if i < N_GROUPS - 1:
                    plan += ["d%d" % i] + ["G%d" % (i - 1)] * (i > 0)
            plan += ["d%d" % (N_GROUPS - 1)]
        elif section == 1:
            plan += ["T"] + every("n") + ["R2"]
            for i in groups:
                plan += ["B%d" % i] + ["d%d" % (i - 1)] * (i > 0)
            plan += ["d%d" % (N_GROUPS - 1), "N", "U"]
        else:
            plan += ["R2"]
            for i in groups:
                plan += ["B%d" % i, "n%d" % i] + ["d%d" % (i - 1)] * (i > 0)
            plan += ["d%d" % (N_GROUPS - 1), "N", "U"]
        plan += [name for name in every("G") if name not in plan]
    plan += ["E"]
    return [name for name in plan if name not in ["d%d" % i for i in DIRECT]]


def kernel(
    order, inputs, weight_hbm, gain, cotangent, left_hbm, right_hbm, out,
    w, wt, h_in, h_sib, h_out, normed, pre, slope, scales, g_in, g_out, dns_out, dns_in, stat_out, stat_in, dpre,
    nrm, dpa, total, stage, frag_out, frag_mid, packed, roots, blocks,
    w_sem, io_sem, stage_sem, yf_s, yf_r, sh_s, sh_r, yb_s, yb_r, dn_s, dn_r, st_s, st_r,
    nr_s, nr_r, ns_s, ns_r, dp_s, dp_r, ds_s, ds_r, sn_s, sn_r, r1_s, r1_r, r2_s, r2_r, fin_s, fin_r,
):
    y = lax.axis_index("pipe")
    k = lax.axis_index("dp")
    t = lax.axis_index("tensor")
    x, z = k // 4, lax.rem(k, 4)
    half = w.shape[1]
    width = w.shape[0]
    block = 512
    frag_rows = 80
    sibling = {"tensor": 1 - t}
    up = {"pipe": lax.rem(y + 1, 4)}
    down = {"pipe": lax.rem(y + 3, 4)}

    def peer(j):
        px = lax.rem(x + j // 4, 4)
        pz = lax.rem(z + lax.rem(j, 4), 4)
        return px, pz, {"dp": px * 4 + pz}

    own0 = pl.multiple_of(t * half, half)
    oth0 = pl.multiple_of((1 - t) * half, half)

    def w_copy(c):
        start = jnp.where(c < N_CHUNKS, own0, oth0) + lax.rem(c, N_CHUNKS) * CHUNK
        rows = pl.ds(pl.multiple_of(start, CHUNK), CHUNK)
        return pltpu.make_async_copy(weight_hbm.at[rows], w.at[rows], w_sem.at[c])

    def stage_copy(i):
        source = (left_hbm, right_hbm)[i % 2]
        return pltpu.make_async_copy(source.at[i // 2], stage.at[i % 2], stage_sem.at[i])

    in_copy = pltpu.make_async_copy(inputs, h_in, io_sem.at[0])
    cot_copy = pltpu.make_async_copy(cotangent, g_in, io_sem.at[1])

    @pl.when(y == 0)
    def _():
        in_copy.start()

    @pl.when(y == 3)
    def _():
        cot_copy.start()

    for i in range(2):
        stage_copy(i).start()
    each(0, 2 * N_CHUNKS, lambda c: w_copy(c).start())

    barrier = pltpu.get_barrier_semaphore()
    for target in (sibling, up, down):
        pl.semaphore_signal(barrier, inc=1, device_id=target, device_id_type=MESH)
    each(1, 16, lambda j: pl.semaphore_signal(barrier, inc=1, device_id=peer(j)[2], device_id_type=MESH))
    pl.semaphore_wait(barrier, 18)

    def cols(c):
        return pl.ds(c * CHUNK, CHUNK)

    def forward_copy(i, c):
        off, m = GROUPS[i]
        n = i * N_CHUNKS + c
        rows = pl.ds(off, m)
        return remote(h_out.at[rows, cols(c)], h_in.at[rows, cols(c)], yf_s.at[n], yf_r.at[n], up)

    def share_copy(i, c):
        off, m = GROUPS[i]
        n = i * N_CHUNKS + c
        rows = pl.ds(off, m)
        return remote(h_in.at[rows, cols(c)], h_sib.at[rows, cols(c)], sh_s.at[n], sh_r.at[n], sibling)

    def backward_copy(i, c):
        off, m = GROUPS[i]
        n = i * N_CHUNKS + c
        rows = pl.ds(off, m)
        return remote(g_out.at[rows, cols(c)], g_in.at[rows, cols(c)], yb_s.at[n], yb_r.at[n], down)

    def dnorm_copy(i, c):
        off, m = GROUPS[i]
        n = i * N_CHUNKS + c
        rows = pl.ds(off, m)
        return remote(dns_out.at[rows, cols(c)], dns_in.at[rows, cols(c)], dn_s.at[n], dn_r.at[n], sibling)

    def stat_copy(i):
        rows = pl.ds(*GROUPS[i])
        return remote(stat_out.at[rows], stat_in.at[rows], st_s.at[i], st_r.at[i], sibling)

    own_band = pl.ds(pl.multiple_of(t * block, block), block)

    def normed_copy(i, d):
        px, pz, target = peer(4 * d)
        columns = pl.ds(pl.multiple_of((2 * px + t) * block, block), block)
        n = i * 4 + d
        return remote(
            normed.at[pl.ds(*GROUPS[i]), columns], nrm[i].at[d, 0, :, own_band], nr_s.at[n], nr_r.at[n], target
        )

    def normed_spread(i, d):
        n = i * 4 + d
        return remote(
            nrm[i].at[:, 0, :, own_band], nrm[i].at[:, d, :, own_band], ns_s.at[n], ns_r.at[n], peer(d)[2]
        )

    def relay_copy(i):
        part = nrm[i].at[:, :, :, own_band]
        return remote(part, part, sn_s.at[i], sn_r.at[i], sibling)

    def dpre_copy(i, j):
        px, pz, target = peer(j)
        columns = pl.ds(pl.multiple_of(pz * block, block), block)
        n = i * 16 + j
        return remote(
            dpre.at[pl.ds(*GROUPS[i]), columns], dpa[i].at[j // 4, lax.rem(j, 4)], dp_s.at[n], dp_r.at[n], target
        )

    def dpre_spread(i, d):
        n = i * 4 + d
        return remote(dpa[i].at[0], dpa[i].at[d], ds_s.at[n], ds_r.at[n], peer(4 * d)[2])

    def dpre_peers(i):
        return 16 if i in DIRECT else 4

    def scatter_copy(j):
        px, pz, target = peer(j)
        return remote(
            frag_out.at[px * 4 + pz], frag_mid.at[pl.ds(2 * k, 2)], r1_s.at[j], r1_r.at[j], target
        )

    def gather_copy(j):
        px, pz, target = peer(j)
        rows = pl.ds(pl.multiple_of(k * frag_rows, frag_rows), frag_rows)
        return remote(frag_out.at[px * 4 + pz], packed.at[:, rows], r2_s.at[j], r2_r.at[j], target)

    def final_copy(d):
        pz = lax.rem(z + d, 4)
        rows = pl.ds(pl.multiple_of(pz * 256, 256), 256)
        columns = pl.ds(pl.multiple_of(z * block, block), block)
        return remote(blocks.at[rows], out.at[:, columns], fin_s.at[d], fin_r.at[d], {"dp": x * 4 + pz})

    def roots_out():
        for i in range(4):
            stage_copy(i).wait()
            values = stage[i % 2].astype(jnp.bfloat16)
            corners = jnp.concatenate([values[128:256, 128:256], values[384:, 384:]], axis=1)
            upper = [values[:128, :256], values[:128, 256:], values[128:256, 256:], values[256:384, 256:], corners]
            first = 8 * (i % 2)
            frag_out[first : first + 8, i // 2] = jnp.concatenate(upper, axis=0).reshape(8, frag_rows, 256)
            if i < 2:
                stage_copy(i + 2).start()
        each(1, 16, lambda j: scatter_copy(j).start())
        frag_mid[pl.ds(2 * k, 2)] = frag_out[k]

    def roots_on():
        each(1, 16, lambda j: scatter_copy(j).wait_send())
        each(1, 16, lambda j: scatter_copy(j).wait_recv())

        def pick(j):
            px, pz, unused = peer(j)
            for i in range(2):
                slot = order[(2 * px + i) * 4 + pz]
                frag_out[px * 4 + pz, i] = frag_mid[slot]

        each(0, 16, pick)
        each(1, 16, lambda j: gather_copy(j).start())
        rows = pl.ds(pl.multiple_of(k * frag_rows, frag_rows), frag_rows)
        packed[:, rows] = frag_out[k]

    def unpack():
        each(1, 16, lambda j: gather_copy(j).wait_recv())

        def one(n):
            i, side = n // 2, lax.rem(n, 2)
            root = roots.at[i, side]
            squares = {}
            for r, (first, second) in enumerate((((0, 0), (0, 1)), ((0, 2), (0, 3)), ((1, 2), (1, 3)), ((2, 2), (2, 3)), ((1, 1), (3, 3)))):
                rows = packed[i, pl.ds(pl.multiple_of(side * 640 + r * 128, 128), 128), :]
                squares[first] = rows[:, :128]
                squares[second] = rows[:, 128:]
            for (a, b), square in squares.items():
                root[a * 128 : a * 128 + 128, b * 128 : b * 128 + 128] = square
                if a != b:
                    root[b * 128 : b * 128 + 128, a * 128 : a * 128 + 128] = square.T

        each(0, 4, one)

    def transpose_weight():
        @pl.when(y >= 2)
        def _():
            each(0, 2 * N_CHUNKS, lambda c: w_copy(c).wait())

        def turn(c):
            part = pl.ds(pl.multiple_of(c * 256, 256), 256)
            wt[:, part] = w[part, :].T

        each(0, width // 256, turn)

    def forward(i):
        off, m = GROUPS[i]
        rows = pl.ds(off, m)
        if i == 0:
            @pl.when(y == 0)
            def _():
                in_copy.wait()
        squares = jnp.zeros((m, 1), jnp.float32)
        for c in range(N_CHUNKS):
            @pl.when(y > 0)
            def _():
                forward_copy(i, c).wait_recv()

            share_copy(i, c).start()
            if i == 0:
                @pl.when(y < 2)
                def _():
                    w_copy(c).wait()
            states = h_in[rows, cols(c)].astype(jnp.float32)
            squares += jnp.sum(states * states, axis=1, keepdims=True)
            place = pl.multiple_of(own0 + c * CHUNK, CHUNK)
            gained = (states * gain[:, pl.ds(place, CHUNK)]).astype(jnp.bfloat16)
            product = jnp.dot(gained, w[pl.ds(place, CHUNK), :], preferred_element_type=jnp.float32)
            pre[rows, :] = product if c == 0 else pre[rows, :] + product
        for c in range(N_CHUNKS):
            share_copy(i, c).wait_recv()
            if i == 0:
                @pl.when(y < 2)
                def _():
                    w_copy(N_CHUNKS + c).wait()
            states = h_sib[rows, cols(c)].astype(jnp.float32)
            squares += jnp.sum(states * states, axis=1, keepdims=True)
            place = pl.multiple_of(oth0 + c * CHUNK, CHUNK)
            gained = (states * gain[:, pl.ds(place, CHUNK)]).astype(jnp.bfloat16)
            if c < N_CHUNKS - 1:
                product = jnp.dot(gained, w[pl.ds(place, CHUNK), :], preferred_element_type=jnp.float32)
                pre[rows, :] += product
        scale = lax.rsqrt(squares / width + norm_eps)
        scales[rows, :] = jnp.broadcast_to(scale, (m, 128))
        for c in range(N_CHUNKS):
            product = jnp.dot(gained, w[pl.ds(place, CHUNK), cols(c)], preferred_element_type=jnp.float32)
            value = scale * (pre[rows, cols(c)] + product)
            logistic = 1.0 / (1.0 + jnp.exp(-value))
            h_out[rows, cols(c)] = (h_in[rows, cols(c)].astype(jnp.float32) + value * logistic).astype(jnp.bfloat16)

            @pl.when(y < 3)
            def _():
                forward_copy(i, c).start()

            pre[rows, cols(c)] = value
            slope[rows, cols(c)] = logistic * (1.0 + value * (1.0 - logistic))

    def normalise(i):
        off, m = GROUPS[i]
        rows = pl.ds(off, m)
        scale = scales[rows, 0:1]
        for c in range(N_CHUNKS):
            for source, first in ((h_in, own0), (h_sib, oth0)):
                columns = pl.ds(pl.multiple_of(first + c * CHUNK, CHUNK), CHUNK)
                states = source[rows, cols(c)].astype(jnp.float32)
                normed[rows, columns] = (states * scale * gain[:, columns]).astype(jnp.bfloat16)
        each(1, 4, lambda d: normed_copy(i, d).start())
        nrm[i][0, 0, :, own_band] = normed[rows, pl.ds(pl.multiple_of((2 * x + t) * block, block), block)]

    def normed_on(i):
        each(1, 4, lambda d: normed_copy(i, d).wait_recv())
        each(1, 4, lambda d: normed_spread(i, d).start())

    def backward(i):
        off, m = GROUPS[i]
        rows = pl.ds(off, m)
        if i == 0:
            @pl.when(y == 3)
            def _():
                cot_copy.wait()
        stat = jnp.zeros((m, 1), jnp.float32)
        for c in range(N_CHUNKS):
            @pl.when(y < 3)
            def _():
                backward_copy(i, c).wait_recv()

            grads = (g_in[rows, cols(c)].astype(jnp.float32) * slope[rows, cols(c)]).astype(jnp.bfloat16)
            dpre[rows, cols(c)] = grads
            stat += jnp.sum(grads.astype(jnp.float32) * pre[rows, cols(c)], axis=1, keepdims=True)

        @pl.when(y > 0)
        def _():
            stat_out[rows, :] = jnp.broadcast_to(stat, (m, 128))
            stat_copy(i).start()

        each(1, dpre_peers(i), lambda j: dpre_copy(i, j).start())
        dpa[i][0, 0] = dpre[rows, pl.ds(pl.multiple_of(z * block, block), block)]

        @pl.when(y > 0)
        def _():
            for c in range(N_CHUNKS):
                columns = pl.ds(pl.multiple_of(oth0 + c * CHUNK, CHUNK), CHUNK)
                part = jnp.dot(dpre[rows, :], wt[:, columns], preferred_element_type=jnp.float32)
                dns_out[rows, cols(c)] = part.astype(jnp.bfloat16)
                dnorm_copy(i, c).start()
            stat_copy(i).wait_recv()
            scale = scales[rows, 0:1]
            mean = (stat_out[rows, 0:1] + stat_in[rows, 0:1]) / width
            for c in range(N_CHUNKS):
                columns = pl.ds(pl.multiple_of(own0 + c * CHUNK, CHUNK), CHUNK)
                part = jnp.dot(dpre[rows, :], wt[:, columns], preferred_element_type=jnp.float32)
                dnorm_copy(i, c).wait_recv()
                part += dns_in[rows, cols(c)].astype(jnp.float32)
                states = h_in[rows, cols(c)].astype(jnp.float32)
                dstates = scale * (part * gain[:, columns] - states * scale * mean)
                g_out[rows, cols(c)] = (g_in[rows, cols(c)].astype(jnp.float32) + dstates).astype(jnp.bfloat16)
                backward_copy(i, c).start()

    def dpre_on(i):
        each(1, dpre_peers(i), lambda j: dpre_copy(i, j).wait_recv())
        each(1, 4, lambda d: dpre_spread(i, d).start())

    def relay():
        for i in range(N_GROUPS):
            each(1, 4, lambda d: normed_spread(i, d).wait_recv())
            relay_copy(i).start()

    def gradient(i):
        m = GROUPS[i][1]
        relay_copy(i).wait_recv()
        if i in DIRECT:
            each(1, 16, lambda j: dpre_copy(i, j).wait_recv())
        else:
            each(1, 4, lambda d: dpre_spread(i, d).wait_recv())
        right = dpa[i][...].reshape(16 * m, block)
        for c in range(4):
            part = pl.ds(c * 256, 256)
            left = nrm[i][:, :, :, part].reshape(16 * m, 256)
            product = lax.dot_general(left, right, (((0,), (0,)), ((), ())), preferred_element_type=jnp.float32)
            total[part, :] = product if i == 0 else total[part, :] + product

    def precondition():
        for i in range(2):
            grad = total[pl.ds(i * block, block), :].astype(jnp.bfloat16)
            lefted = jnp.dot(roots[i, 0], grad, preferred_element_type=jnp.float32).astype(jnp.bfloat16)
            result = jnp.dot(lefted, roots[i, 1], preferred_element_type=jnp.float32).astype(jnp.bfloat16)
            blocks[pl.ds(i * block, block), :] = result
            for d in range(1, 4):
                @pl.when(lax.rem(z + d, 4) // 2 == i)
                def _():
                    final_copy(d).start()
        columns = pl.ds(pl.multiple_of(z * block, block), block)
        out[:, columns] = blocks[pl.ds(pl.multiple_of(z * 256, 256), 256), :]

        for i in range(N_GROUPS):
            for c in range(N_CHUNKS):
                share_copy(i, c).wait_send()

                @pl.when(y < 3)
                def _():
                    forward_copy(i, c).wait_send()

                @pl.when(y > 0)
                def _():
                    backward_copy(i, c).wait_send()
                    dnorm_copy(i, c).wait_send()

            @pl.when(y > 0)
            def _():
                stat_copy(i).wait_send()

            relay_copy(i).wait_send()
            each(1, 4, lambda d: normed_copy(i, d).wait_send())
            each(1, 4, lambda d: normed_spread(i, d).wait_send())
            each(1, dpre_peers(i), lambda j: dpre_copy(i, j).wait_send())
            if i not in DIRECT:
                each(1, 4, lambda d: dpre_spread(i, d).wait_send())
        each(1, 16, lambda j: gather_copy(j).wait_send())
        for d in range(1, 4):
            final_copy(d).wait_send()
        for d in range(1, 4):
            final_copy(d).wait_recv()

    ops = dict(R1=roots_out, R2=roots_on, U=unpack, T=transpose_weight, N=relay, E=precondition)
    kinds = dict(F=forward, X=normalise, n=normed_on, B=backward, d=dpre_on, G=gradient)
    for i in range(N_GROUPS):
        for kind, op in kinds.items():
            if kind != "d" or i not in DIRECT:
                ops[kind + str(i)] = functools.partial(op, i)
    plans = [plan_of(section) for section in range(4)]

    def step(s):
        for name, op in ops.items():
            place = [plan.index(name) if name in plan else -1 for plan in plans]
            mine = jnp.int32(place[3])
            for section in (2, 1, 0):
                mine = jnp.where(y == section, place[section], mine)
            pl.when(s == mine)(op)

    each(0, max(len(plan) for plan in plans), step)


def on_device(inputs, weights, norm_gains, cotangent, owner_table, left_roots, right_roots):
    tokens = inputs.shape[0] * inputs.shape[1]
    half = weights.shape[2]
    width = weights.shape[1]
    bf16, f32 = jnp.bfloat16, jnp.float32
    vmem, dma = pltpu.VMEM, pltpu.SemaphoreType.DMA
    steps = N_GROUPS * N_CHUNKS
    scratch = [
        vmem((width, half), bf16), vmem((half, width), bf16),
        vmem((tokens, half), bf16), vmem((tokens, half), bf16), vmem((tokens, half), bf16),
        vmem((tokens, width), bf16), vmem((tokens, half), f32), vmem((tokens, half), f32), vmem((tokens, 128), f32),
        vmem((tokens, half), bf16), vmem((tokens, half), bf16), vmem((tokens, half), bf16), vmem((tokens, half), bf16),
        vmem((tokens, 128), f32), vmem((tokens, 128), f32), vmem((tokens, half), bf16),
        [vmem((4, 4, m, 1024), bf16) for unused, m in GROUPS], [vmem((4, 4, m, 512), bf16) for unused, m in GROUPS],
        vmem((1024, 512), f32), vmem((2, 512, 512), f32),
        vmem((16, 2, 80, 256), bf16), vmem((32, 80, 256), bf16), vmem((2, 1280, 256), bf16),
        vmem((2, 2, 512, 512), bf16),
        vmem((1024, 512), bf16),
        dma((8,)), dma((2,)), dma((4,)),
        dma((steps,)), dma((steps,)), dma((steps,)), dma((steps,)),
        dma((steps,)), dma((steps,)), dma((steps,)), dma((steps,)), dma((N_GROUPS,)), dma((N_GROUPS,)),
        dma((N_GROUPS * 4,)), dma((N_GROUPS * 4,)), dma((N_GROUPS * 4,)), dma((N_GROUPS * 4,)),
        dma((N_GROUPS * 16,)), dma((N_GROUPS * 16,)), dma((N_GROUPS * 4,)), dma((N_GROUPS * 4,)),
        dma((N_GROUPS,)), dma((N_GROUPS,)),
        dma((16,)), dma((16,)), dma((16,)), dma((16,)), dma((4,)), dma((4,)),
    ]
    in_vmem = pl.BlockSpec(memory_space=pltpu.VMEM)
    in_hbm = pl.BlockSpec(memory_space=pl.ANY)
    result = pl.pallas_call(
        kernel,
        out_shape=jax.ShapeDtypeStruct((256, half), bf16),
        in_specs=[pl.BlockSpec(memory_space=pltpu.SMEM), in_hbm, in_hbm, in_vmem, in_hbm, in_hbm, in_hbm],
        out_specs=in_vmem,
        scratch_shapes=scratch,
        compiler_params=pltpu.CompilerParams(
            collective_id=0, has_side_effects=True, vmem_limit_bytes=62 * 2**20
        ),
    )(
        owner_table.reshape(-1), inputs.reshape(tokens, half), weights[0], norm_gains,
        cotangent.reshape(tokens, half), left_roots[0, 0], right_roots[0, 0],
    )
    return result[None]


def solution(mesh):
    return jax.shard_map(
        on_device,
        mesh=mesh,
        in_specs=(
            P(None, "dp", "tensor"),
            P("pipe", None, "tensor"),
            P("pipe", None),
            P(None, "dp", "tensor"),
            P("pipe", "tensor", None),
            P("pipe", "tensor", "dp", None, None),
            P("pipe", "tensor", "dp", None, None),
        ),
        out_specs=P("pipe", "dp", "tensor"),
        check_vma=False,
    )
```

time: 1060 us -> 123 us (0.12)
  the two profiles are of different devices: /device:TPU:100 before, /device:TPU:10 now
where the time goes in v1:
time: 123 us
  Pallas kernels  120 us (98%)
  local copies, waits for them, and re-layouts  2.3 us (2%)
    pallas_call x1, Pallas kernels, on_device(): pl.pallas_call(kernel, out_shape=jax.ShapeDtypeStruct((256, half), bf16),...  120 us

profile of v1, /device:TPU:10, one launch (start us, length us, event | category | flops | bytes accessed | tf_op | source)
XLA Modules:
  0.0 122.6 jit_solution(4295019365227595121)
XLA Ops:
  0.0 120.3 %shard_map.73 = bf16[256,2048]{1,0:T(8,128)(2,1)} custom-call(s32[32]{0:T(128)} %bitcast.13, bf16[128,2048]{1,0:T(8,128)(2,1)} %bitcast.11, bf16[4096,2048]{1,0:T(8,128)(2,1)} %bitcast.7, f32[1,4096]{1,0:T(1,128)} %gain.1, bf16[128,2048]{1,0:T(8,128)(2,1)} %bitcast.12, f32[2,512,512]{2,1,0:T(8,128)} %bitcast.9, f32[2,512,512]{2,1,0:T(8,128)} %bitcast.10), custom_call_target="tpu_custom_call" | custom-call | tf_op jit(solution)/shard_map/pallas_call | solution.py:495
  120.3 2.3 %copy.9 = bf16[1,256,2048]{2,1,0:T(8,128)(2,1)} copy(bf16[1,256,2048]{2,1,0:T(8,128)(2,1)} %bitcast.8) | data formatting | bytes 2097152

commit v2 on v1

--- a/solution.py
+++ b/solution.py
@@ -13,7 +13,7 @@
 N_GROUPS = len(GROUPS)
 CHUNK = 512
 N_CHUNKS = 4
-DIRECT = (N_GROUPS - 1,)
+DIRECT = (1, 2)
 
 
 def remote(src, dst, send, recv, target):
@@ -36,46 +36,51 @@
     def every(kind):
         return [kind + str(i) for i in groups]
 
-    plan = ["R1"] + ["T"] * (section >= 2)
-    if section == 3:
+    if section == 0:
+        plan = ["F0", "X0", "R1"]
+        for i in groups[1:]:
+            plan += ["F%d" % i, "X%d" % i, "n%d" % (i - 1)]
+        plan += ["n%d" % (N_GROUPS - 1), "R2"] + every("N")
         for i in groups:
-            plan += ["F%d" % i, "B%d" % i]
-            plan += ["R2"] * (i == 0)
-            plan += ["X%d" % i]
+            plan += ["B%d" % i]
+            if i < N_GROUPS - 1:
+                plan += ["d%d" % i] + ["G%d" % (i - 1)] * (i > 0)
+            if i == N_GROUPS - 2:
+                plan += ["U"]
+        plan += ["d%d" % (N_GROUPS - 1)]
+    elif section == 1:
+        plan = ["R1"]
         for i in groups:
-            plan += ["d%d" % i, "n%d" % i]
-        plan += ["N", "U"] + every("G")
+            plan += ["F%d" % i, "X%d" % i] + (["n%d" % (i - 1)] if i > 0 else ["R2"])
+        plan += ["n%d" % (N_GROUPS - 1), "T"]
+        for i in groups:
+            plan += ["B%d" % i, "d%d" % i]
+        plan += every("N") + ["U"]
+    elif section == 2:
+        plan = ["R1", "T"]
+        for i in groups:
+            plan += ["F%d" % i, "X%d" % i] + ["R2"] * (i == 0)
+        for i in groups:
+            plan += ["B%d" % i, "n%d" % i] + ["d%d" % (i - 1)] * (i > 0)
+        plan += ["d%d" % (N_GROUPS - 1)] + every("N") + ["U"]
     else:
+        plan = ["R1", "T", "R2"]
         for i in groups:
-            plan += ["F%d" % i, "X%d" % i]
-        if section == 0:
-            plan += every("n") + ["R2", "N", "U"]
-            for i in groups:
-                plan += ["B%d" % i]
-                if i < N_GROUPS - 1:
-                    plan += ["d%d" % i] + ["G%d" % (i - 1)] * (i > 0)
-            plan += ["d%d" % (N_GROUPS - 1)]
-        elif section == 1:
-            plan += ["T"] + every("n") + ["R2"]
-            for i in groups:
-                plan += ["B%d" % i] + ["d%d" % (i - 1)] * (i > 0)
-            plan += ["d%d" % (N_GROUPS - 1), "N", "U"]
-        else:
-            plan += ["R2"]
-            for i in groups:
-                plan += ["B%d" % i, "n%d" % i] + ["d%d" % (i - 1)] * (i > 0)
-            plan += ["d%d" % (N_GROUPS - 1), "N", "U"]
-        plan += [name for name in every("G") if name not in plan]
+            plan += ["F%d" % i, "B%d" % i, "X%d" % i]
+            if i > 0:
+                plan += ["n%d" % (i - 1), "d%d" % (i - 1)]
+        plan += ["n%d" % (N_GROUPS - 1), "d%d" % (N_GROUPS - 1)] + every("N") + ["U"]
+    plan += [name for name in every("G") if name not in plan]
     plan += ["E"]
     return [name for name in plan if name not in ["d%d" % i for i in DIRECT]]
 
 
 def kernel(
-    order, inputs, weight_hbm, gain, cotangent, left_hbm, right_hbm, out,
+    order, inputs, weight_hbm, gain, cotangent, left_hbm, right_hbm, out_left, out_right,
     w, wt, h_in, h_sib, h_out, normed, pre, slope, scales, g_in, g_out, dns_out, dns_in, stat_out, stat_in, dpre,
-    nrm, dpa, total, stage, frag_out, frag_mid, packed, roots, blocks,
+    nrm, dpa, total, stage, frag_out, frag_mid, diag_mid, packed, roots, blocks,
     w_sem, io_sem, stage_sem, yf_s, yf_r, sh_s, sh_r, yb_s, yb_r, dn_s, dn_r, st_s, st_r,
-    nr_s, nr_r, ns_s, ns_r, dp_s, dp_r, ds_s, ds_r, sn_s, sn_r, r1_s, r1_r, r2_s, r2_r, fin_s, fin_r,
+    nr_s, nr_r, ns_s, ns_r, dp_s, dp_r, ds_s, ds_r, sn_s, sn_r, r1_s, r1_r, rd_s, rd_r, r2_s, r2_r, fin_s, fin_r,
 ):
     y = lax.axis_index("pipe")
     k = lax.axis_index("dp")
@@ -84,7 +89,7 @@
     half = w.shape[1]
     width = w.shape[0]
     block = 512
-    frag_rows = 80
+    frag_rows = 64
     sibling = {"tensor": 1 - t}
     up = {"pipe": lax.rem(y + 1, 4)}
     down = {"pipe": lax.rem(y + 3, 4)}
@@ -117,9 +122,13 @@
     def _():
         cot_copy.start()
 
-    for i in range(2):
-        stage_copy(i).start()
+    def stage_start():
+        for i in range(2):
+            stage_copy(i).start()
+
+    pl.when(y > 0)(stage_start)
     each(0, 2 * N_CHUNKS, lambda c: w_copy(c).start())
+    pl.when(y == 0)(stage_start)
 
     barrier = pltpu.get_barrier_semaphore()
     for target in (sibling, up, down):
@@ -199,33 +208,58 @@
             frag_out.at[px * 4 + pz], frag_mid.at[pl.ds(2 * k, 2)], r1_s.at[j], r1_r.at[j], target
         )
 
+    def diag_copy(j):
+        part = diag_mid.at[pl.ds(2 * k, 2)]
+        return remote(part, part, rd_s.at[j], rd_r.at[j], peer(j)[2])
+
     def gather_copy(j):
         px, pz, target = peer(j)
         rows = pl.ds(pl.multiple_of(k * frag_rows, frag_rows), frag_rows)
         return remote(frag_out.at[px * 4 + pz], packed.at[:, rows], r2_s.at[j], r2_r.at[j], target)
 
-    def final_copy(d):
+    def final_copy(d, out=out_left):
         pz = lax.rem(z + d, 4)
         rows = pl.ds(pl.multiple_of(pz * 256, 256), 256)
-        columns = pl.ds(pl.multiple_of(z * block, block), block)
+        columns = pl.ds(pl.multiple_of(lax.rem(z, 2) * block, block), block)
         return remote(blocks.at[rows], out.at[:, columns], fin_s.at[d], fin_r.at[d], {"dp": x * 4 + pz})
+
+    row_of = lax.broadcasted_iota(jnp.int32, (128, 128), 0)
+    col_of = lax.broadcasted_iota(jnp.int32, (128, 128), 1)
 
     def roots_out():
         for i in range(4):
             stage_copy(i).wait()
             values = stage[i % 2].astype(jnp.bfloat16)
-            corners = jnp.concatenate([values[128:256, 128:256], values[384:, 384:]], axis=1)
-            upper = [values[:128, :256], values[:128, 256:], values[128:256, 256:], values[256:384, 256:], corners]
+
+            def square(a, b):
+                return values[a * 128 : a * 128 + 128, b * 128 : b * 128 + 128]
+
+            def fold(a, b):
+                return jnp.where(col_of >= row_of, square(a, a).astype(jnp.float32), square(b, b).astype(jnp.float32))
+
+            for n in range(2):
+                corner = jnp.where(col_of == row_of, square(2 * n + 1, 2 * n + 1).astype(jnp.float32), 0.0)
+                row = 2 * (i % 2) + n
+                diag_mid[2 * k + i // 2, row : row + 1, :] = jnp.sum(corner, axis=0, keepdims=True)
+            upper = [
+                values[:128, 128:384],
+                jnp.concatenate([square(0, 3), square(1, 2)], axis=1),
+                jnp.concatenate([square(1, 3), square(2, 3)], axis=1),
+                jnp.concatenate([fold(0, 1), fold(2, 3)], axis=1).astype(jnp.bfloat16),
+            ]
             first = 8 * (i % 2)
             frag_out[first : first + 8, i // 2] = jnp.concatenate(upper, axis=0).reshape(8, frag_rows, 256)
             if i < 2:
                 stage_copy(i + 2).start()
         each(1, 16, lambda j: scatter_copy(j).start())
+        each(1, 16, lambda j: diag_copy(j).start())
         frag_mid[pl.ds(2 * k, 2)] = frag_out[k]
 
     def roots_on():
         each(1, 16, lambda j: scatter_copy(j).wait_send())
         each(1, 16, lambda j: scatter_copy(j).wait_recv())
+        each(1, 16, lambda j: diag_copy(j).wait_send())
+        each(1, 16, lambda j: diag_copy(j).wait_recv())
 
         def pick(j):
             px, pz, unused = peer(j)
@@ -244,15 +278,26 @@
         def one(n):
             i, side = n // 2, lax.rem(n, 2)
             root = roots.at[i, side]
-            squares = {}
-            for r, (first, second) in enumerate((((0, 0), (0, 1)), ((0, 2), (0, 3)), ((1, 2), (1, 3)), ((2, 2), (2, 3)), ((1, 1), (3, 3)))):
-                rows = packed[i, pl.ds(pl.multiple_of(side * 640 + r * 128, 128), 128), :]
-                squares[first] = rows[:, :128]
-                squares[second] = rows[:, 128:]
-            for (a, b), square in squares.items():
+            diagonals = diag_mid[order[(2 * x + i) * 4 + z]]
+
+            def place(a, b, square):
                 root[a * 128 : a * 128 + 128, b * 128 : b * 128 + 128] = square
-                if a != b:
-                    root[b * 128 : b * 128 + 128, a * 128 : a * 128 + 128] = square.T
+
+            def rows(r):
+                return packed[i, pl.ds(pl.multiple_of(side * 512 + r * 128, 128), 128), :]
+
+            for r, pair in enumerate((((0, 1), (0, 2)), ((0, 3), (1, 2)), ((1, 3), (2, 3)))):
+                both = rows(r)
+                for (a, b), square in zip(pair, (both[:, :128], both[:, 128:])):
+                    place(a, b, square)
+                    place(b, a, square.T)
+            both = rows(3).astype(jnp.float32)
+            for m, square in enumerate((both[:, :128], both[:, 128:])):
+                turned = square.T
+                place(2 * m, 2 * m, jnp.where(col_of >= row_of, square, turned).astype(jnp.bfloat16))
+                diagonal = jnp.where(side == 0, diagonals[m : m + 1, :], diagonals[m + 2 : m + 3, :])
+                second = jnp.where(col_of < row_of, square, jnp.where(col_of > row_of, turned, diagonal))
+                place(2 * m + 1, 2 * m + 1, second.astype(jnp.bfloat16))
 
         each(0, 4, one)
 
@@ -351,13 +396,18 @@
             grads = (g_in[rows, cols(c)].astype(jnp.float32) * slope[rows, cols(c)]).astype(jnp.bfloat16)
             dpre[rows, cols(c)] = grads
             stat += jnp.sum(grads.astype(jnp.float32) * pre[rows, cols(c)], axis=1, keepdims=True)
+            if i in DIRECT:
+                ahead = lax.rem(c - z + 4, 4)
+                each(1, 4, lambda d: dpre_copy(i, 4 * d + ahead).start())
+                pl.when(ahead > 0)(lambda: dpre_copy(i, ahead).start())
 
         @pl.when(y > 0)
         def _():
             stat_out[rows, :] = jnp.broadcast_to(stat, (m, 128))
             stat_copy(i).start()
 
-        each(1, dpre_peers(i), lambda j: dpre_copy(i, j).start())
+        if i not in DIRECT:
+            each(1, 4, lambda j: dpre_copy(i, j).start())
         dpa[i][0, 0] = dpre[rows, pl.ds(pl.multiple_of(z * block, block), block)]
 
         @pl.when(y > 0)
@@ -384,10 +434,9 @@
         each(1, dpre_peers(i), lambda j: dpre_copy(i, j).wait_recv())
         each(1, 4, lambda d: dpre_spread(i, d).start())
 
-    def relay():
-        for i in range(N_GROUPS):
-            each(1, 4, lambda d: normed_spread(i, d).wait_recv())
-            relay_copy(i).start()
+    def relay(i):
+        each(1, 4, lambda d: normed_spread(i, d).wait_recv())
+        relay_copy(i).start()
 
     def gradient(i):
         m = GROUPS[i][1]
@@ -410,11 +459,18 @@
             result = jnp.dot(lefted, roots[i, 1], preferred_element_type=jnp.float32).astype(jnp.bfloat16)
             blocks[pl.ds(i * block, block), :] = result
             for d in range(1, 4):
-                @pl.when(lax.rem(z + d, 4) // 2 == i)
-                def _():
-                    final_copy(d).start()
-        columns = pl.ds(pl.multiple_of(z * block, block), block)
-        out[:, columns] = blocks[pl.ds(pl.multiple_of(z * 256, 256), 256), :]
+                for side, out in enumerate((out_left, out_right)):
+                    @pl.when((lax.rem(z + d, 4) // 2 == i) & (z // 2 == side))
+                    def _():
+                        final_copy(d, out).start()
+
+        def keep_copy(out):
+            rows = pl.ds(pl.multiple_of(z * 256, 256), 256)
+            columns = pl.ds(pl.multiple_of(lax.rem(z, 2) * block, block), block)
+            return pltpu.make_async_copy(blocks.at[rows], out.at[:, columns], io_sem.at[0])
+
+        for side, out in enumerate((out_left, out_right)):
+            pl.when(z // 2 == side)(lambda: keep_copy(out).start())
 
         for i in range(N_GROUPS):
             for c in range(N_CHUNKS):
@@ -442,11 +498,12 @@
         each(1, 16, lambda j: gather_copy(j).wait_send())
         for d in range(1, 4):
             final_copy(d).wait_send()
+        keep_copy(out_left).wait()
         for d in range(1, 4):
             final_copy(d).wait_recv()
 
-    ops = dict(R1=roots_out, R2=roots_on, U=unpack, T=transpose_weight, N=relay, E=precondition)
-    kinds = dict(F=forward, X=normalise, n=normed_on, B=backward, d=dpre_on, G=gradient)
+    ops = dict(R1=roots_out, R2=roots_on, U=unpack, T=transpose_weight, E=precondition)
+    kinds = dict(F=forward, X=normalise, n=normed_on, N=relay, B=backward, d=dpre_on, G=gradient)
     for i in range(N_GROUPS):
         for kind, op in kinds.items():
             if kind != "d" or i not in DIRECT:
@@ -479,7 +536,7 @@
         vmem((tokens, 128), f32), vmem((tokens, 128), f32), vmem((tokens, half), bf16),
         [vmem((4, 4, m, 1024), bf16) for unused, m in GROUPS], [vmem((4, 4, m, 512), bf16) for unused, m in GROUPS],
         vmem((1024, 512), f32), vmem((2, 512, 512), f32),
-        vmem((16, 2, 80, 256), bf16), vmem((32, 80, 256), bf16), vmem((2, 1280, 256), bf16),
+        vmem((16, 2, 64, 256), bf16), vmem((32, 64, 256), bf16), vmem((32, 8, 128), f32), vmem((2, 1024, 256), bf16),
         vmem((2, 2, 512, 512), bf16),
         vmem((1024, 512), bf16),
         dma((8,)), dma((2,)), dma((4,)),
@@ -488,15 +545,15 @@
         dma((N_GROUPS * 4,)), dma((N_GROUPS * 4,)), dma((N_GROUPS * 4,)), dma((N_GROUPS * 4,)),
         dma((N_GROUPS * 16,)), dma((N_GROUPS * 16,)), dma((N_GROUPS * 4,)), dma((N_GROUPS * 4,)),
         dma((N_GROUPS,)), dma((N_GROUPS,)),
-        dma((16,)), dma((16,)), dma((16,)), dma((16,)), dma((4,)), dma((4,)),
+        dma((16,)), dma((16,)), dma((16,)), dma((16,)), dma((16,)), dma((16,)), dma((4,)), dma((4,)),
     ]
     in_vmem = pl.BlockSpec(memory_space=pltpu.VMEM)
     in_hbm = pl.BlockSpec(memory_space=pl.ANY)
     result = pl.pallas_call(
         kernel,
-        out_shape=jax.ShapeDtypeStruct((256, half), bf16),
+        out_shape=[jax.ShapeDtypeStruct((256, half // 2), bf16)] * 2,
         in_specs=[pl.BlockSpec(memory_space=pltpu.SMEM), in_hbm, in_hbm, in_vmem, in_hbm, in_hbm, in_hbm],
-        out_specs=in_vmem,
+        out_specs=[in_hbm, in_hbm],
         scratch_shapes=scratch,
         compiler_params=pltpu.CompilerParams(
             collective_id=0, has_side_effects=True, vmem_limit_bytes=62 * 2**20
@@ -505,7 +562,7 @@
         owner_table.reshape(-1), inputs.reshape(tokens, half), weights[0], norm_gains,
         cotangent.reshape(tokens, half), left_roots[0, 0], right_roots[0, 0],
     )
-    return result[None]
+    return jnp.concatenate(result, axis=1)[None]
 
 
 def solution(mesh):

time: 123 us -> 114 us (0.927)
  the two profiles are of different devices: /device:TPU:10 before, /device:TPU:66 now
where the time goes in v2:
time: 114 us; the launch traced here: 111 us
  Pallas kernels  109 us (96%)
  other arithmetic  2.27 us (2%)
    pallas_call x1, Pallas kernels, on_device(): pl.pallas_call(kernel, out_shape=[jax.ShapeDtypeStruct((256, half // 2),...  109 us

profile of v2, /device:TPU:66, one launch (start us, length us, event | category | flops | bytes accessed | tf_op | source)
XLA Modules:
  0.0 111.4 jit_solution(5743354818858604673)
XLA Ops:
  0.0 109.2 %shard_map.73 = (bf16[256,1024]{1,0:T(8,128)(2,1)}, bf16[256,1024]{1,0:T(8,128)(2,1)}) custom-call(s32[32]{0:T(128)} %bitcast.13, bf16[128,2048]{1,0:T(8,128)(2,1)} %bitcast.11, bf16[4096,2048]{1,0:T(8,128)(2,1)} %bitcast.8, f32[1,4096]{1,0:T(1,128)} %gain.1, bf16[128,2048]{1,0:T(8,128)(2,1)} %bitcast.12, f32[2,512,512]{2,1,0:T(8,128)} %bitcast.9, ...), custom_call_target="tpu_custom_call" | custom-call | tf_op jit(solution)/shard_map/pallas_call | solution.py:552
  109.2 2.3 %maximum_bitcast_fusion = bf16[1,256,2048]{2,1,0:T(8,128)(2,1)} fusion(bf16[256,1024]{1,0:T(8,128)(2,1)} %get-tuple-element.8, bf16[256,1024]{1,0:T(8,128)(2,1)} %get-tuple-element.7), kind=kLoop, calls=%fused_computation | loop fusion | flops 2097152 | bytes 2097152 | tf_op jit(solution)/shard_map/broadcast_in_dim | solution.py:565

commit v3 on v2

--- a/solution.py
+++ b/solution.py
@@ -14,6 +14,7 @@
 CHUNK = 512
 N_CHUNKS = 4
 DIRECT = (1, 2)
+RING = (0, 1, 2)
 
 
 def remote(src, dst, send, recv, target):
@@ -40,7 +41,7 @@
         plan = ["F0", "X0", "R1"]
         for i in groups[1:]:
             plan += ["F%d" % i, "X%d" % i, "n%d" % (i - 1)]
-        plan += ["n%d" % (N_GROUPS - 1), "R2"] + every("N")
+        plan += ["R2", "n%d" % (N_GROUPS - 1)] + every("m") + every("N")
         for i in groups:
             plan += ["B%d" % i]
             if i < N_GROUPS - 1:
@@ -52,7 +53,7 @@
         plan = ["R1"]
         for i in groups:
             plan += ["F%d" % i, "X%d" % i] + (["n%d" % (i - 1)] if i > 0 else ["R2"])
-        plan += ["n%d" % (N_GROUPS - 1), "T"]
+        plan += ["n%d" % (N_GROUPS - 1), "m0", "T"] + every("m")[1:]
         for i in groups:
             plan += ["B%d" % i, "d%d" % i]
         plan += every("N") + ["U"]
@@ -61,18 +62,23 @@
         for i in groups:
             plan += ["F%d" % i, "X%d" % i] + ["R2"] * (i == 0)
         for i in groups:
-            plan += ["B%d" % i, "n%d" % i] + ["d%d" % (i - 1)] * (i > 0)
-        plan += ["d%d" % (N_GROUPS - 1)] + every("N") + ["U"]
+            plan += ["B%d" % i] + ["m%d" % (i - 1)] * (i > 0) + ["n%d" % i] + ["d%d" % (i - 1)] * (i > 0)
+        plan += ["d%d" % (N_GROUPS - 1), "U", "m%d" % (N_GROUPS - 1)] + every("N")
     else:
         plan = ["R1", "T", "R2"]
         for i in groups:
-            plan += ["F%d" % i, "B%d" % i, "X%d" % i]
+            if i < N_GROUPS - 1:
+                plan += ["F%d" % i, "B%d" % i, "X%d" % i]
+            else:
+                plan += ["F%d" % i, "X%d" % i, "B%d" % i]
             if i > 0:
-                plan += ["n%d" % (i - 1), "d%d" % (i - 1)]
-        plan += ["n%d" % (N_GROUPS - 1), "d%d" % (N_GROUPS - 1)] + every("N") + ["U"]
+                plan += ["m%d" % (i - 2)] * (i > 1) + ["n%d" % (i - 1), "d%d" % (i - 1)]
+        last = N_GROUPS - 1
+        plan += ["U", "n%d" % last, "d%d" % last, "m%d" % (last - 1), "m%d" % last] + every("N")
     plan += [name for name in every("G") if name not in plan]
     plan += ["E"]
-    return [name for name in plan if name not in ["d%d" % i for i in DIRECT]]
+    without = ["d%d" % i for i in DIRECT] + ["m%d" % i for i in groups if i not in RING]
+    return [name for name in plan if name not in without]
 
 
 def kernel(
@@ -80,7 +86,7 @@
     w, wt, h_in, h_sib, h_out, normed, pre, slope, scales, g_in, g_out, dns_out, dns_in, stat_out, stat_in, dpre,
     nrm, dpa, total, stage, frag_out, frag_mid, diag_mid, packed, roots, blocks,
     w_sem, io_sem, stage_sem, yf_s, yf_r, sh_s, sh_r, yb_s, yb_r, dn_s, dn_r, st_s, st_r,
-    nr_s, nr_r, ns_s, ns_r, dp_s, dp_r, ds_s, ds_r, sn_s, sn_r, r1_s, r1_r, rd_s, rd_r, r2_s, r2_r, fin_s, fin_r,
+    nr_s, nr_r, ns_s, ns_r, nh_s, nh_r, dp_s, dp_r, ds_s, ds_r, sn_s, sn_r, r1_s, r1_r, rd_s, rd_r, r2_s, r2_r, fin_s, fin_r,
 ):
     y = lax.axis_index("pipe")
     k = lax.axis_index("dp")
@@ -181,6 +187,16 @@
         n = i * 4 + d
         return remote(
             nrm[i].at[:, 0, :, own_band], nrm[i].at[:, d, :, own_band], ns_s.at[n], ns_r.at[n], peer(d)[2]
+        )
+
+    def spread_ways(i):
+        return (1, 3) if i in RING else (1, 2, 3)
+
+    def normed_hand_on(i, d):
+        half_band = pl.ds(pl.multiple_of(t * block + (d // 2) * (block // 2), block // 2), block // 2)
+        n = i * 4 + d
+        return remote(
+            nrm[i].at[:, d, :, half_band], nrm[i].at[:, 2, :, half_band], nh_s.at[n], nh_r.at[n], peer(d)[2]
         )
 
     def relay_copy(i):
@@ -378,7 +394,13 @@
 
     def normed_on(i):
         each(1, 4, lambda d: normed_copy(i, d).wait_recv())
-        each(1, 4, lambda d: normed_spread(i, d).start())
+        for d in spread_ways(i):
+            normed_spread(i, d).start()
+
+    def normed_round(i):
+        for d in (1, 3):
+            normed_spread(i, d).wait_recv()
+            normed_hand_on(i, d).start()
 
     def backward(i):
         off, m = GROUPS[i]
@@ -435,7 +457,11 @@
         each(1, 4, lambda d: dpre_spread(i, d).start())
 
     def relay(i):
-        each(1, 4, lambda d: normed_spread(i, d).wait_recv())
+        if i in RING:
+            for d in (1, 3):
+                normed_hand_on(i, d).wait_recv()
+        else:
+            each(1, 4, lambda d: normed_spread(i, d).wait_recv())
         relay_copy(i).start()
 
     def gradient(i):
@@ -491,7 +517,11 @@
 
             relay_copy(i).wait_send()
             each(1, 4, lambda d: normed_copy(i, d).wait_send())
-            each(1, 4, lambda d: normed_spread(i, d).wait_send())
+            for d in spread_ways(i):
+                normed_spread(i, d).wait_send()
+            if i in RING:
+                for d in (1, 3):
+                    normed_hand_on(i, d).wait_send()
             each(1, dpre_peers(i), lambda j: dpre_copy(i, j).wait_send())
             if i not in DIRECT:
                 each(1, 4, lambda d: dpre_spread(i, d).wait_send())
@@ -503,10 +533,10 @@
             final_copy(d).wait_recv()
 
     ops = dict(R1=roots_out, R2=roots_on, U=unpack, T=transpose_weight, E=precondition)
-    kinds = dict(F=forward, X=normalise, n=normed_on, N=relay, B=backward, d=dpre_on, G=gradient)
+    kinds = dict(F=forward, X=normalise, n=normed_on, m=normed_round, N=relay, B=backward, d=dpre_on, G=gradient)
     for i in range(N_GROUPS):
         for kind, op in kinds.items():
-            if kind != "d" or i not in DIRECT:
+            if (kind != "d" or i not in DIRECT) and (kind != "m" or i in RING):
                 ops[kind + str(i)] = functools.partial(op, i)
     plans = [plan_of(section) for section in range(4)]
 
@@ -543,6 +573,7 @@
         dma((steps,)), dma((steps,)), dma((steps,)), dma((steps,)),
         dma((steps,)), dma((steps,)), dma((steps,)), dma((steps,)), dma((N_GROUPS,)), dma((N_GROUPS,)),
         dma((N_GROUPS * 4,)), dma((N_GROUPS * 4,)), dma((N_GROUPS * 4,)), dma((N_GROUPS * 4,)),
+        dma((N_GROUPS * 4,)), dma((N_GROUPS * 4,)),
         dma((N_GROUPS * 16,)), dma((N_GROUPS * 16,)), dma((N_GROUPS * 4,)), dma((N_GROUPS * 4,)),
         dma((N_GROUPS,)), dma((N_GROUPS,)),
         dma((16,)), dma((16,)), dma((16,)), dma((16,)), dma((16,)), dma((16,)), dma((4,)), dma((4,)),

time: 114 us -> 113 us (level); the launches traced: 111 us -> 112 us
  no operation moved by 1% of the time
where the time goes in v3:
time: 113 us; the launch traced here: 112 us
  Pallas kernels  110 us (97%)
  other arithmetic  2.27 us (2%)
    pallas_call x1, Pallas kernels, on_device(): pl.pallas_call(kernel, out_shape=[jax.ShapeDtypeStruct((256, half // 2),...  110 us
    broadcast_in_dim x1, other arithmetic, on_device(): return jnp.concatenate(result, axis=1)[None]  2.27 us

profile of v3, /device:TPU:66, one launch (start us, length us, event | category | flops | bytes accessed | tf_op | source)
XLA Modules:
  0.0 112.5 jit_solution(10869158609232488932)
XLA Ops:
  0.0 110.2 %shard_map.73 = (bf16[256,1024]{1,0:T(8,128)(2,1)}, bf16[256,1024]{1,0:T(8,128)(2,1)}) custom-call(s32[32]{0:T(128)} %bitcast.13, bf16[128,2048]{1,0:T(8,128)(2,1)} %bitcast.11, bf16[4096,2048]{1,0:T(8,128)(2,1)} %bitcast.8, f32[1,4096]{1,0:T(1,128)} %gain.1, bf16[128,2048]{1,0:T(8,128)(2,1)} %bitcast.12, f32[2,512,512]{2,1,0:T(8,128)} %bitcast.9, ...), custom_call_target="tpu_custom_call" | custom-call | tf_op jit(solution)/shard_map/pallas_call | solution.py:583
  110.2 2.3 %maximum_bitcast_fusion = bf16[1,256,2048]{2,1,0:T(8,128)(2,1)} fusion(bf16[256,1024]{1,0:T(8,128)(2,1)} %get-tuple-element.8, bf16[256,1024]{1,0:T(8,128)(2,1)} %get-tuple-element.7), kind=kLoop, calls=%fused_computation | loop fusion | flops 2097152 | bytes 2097152 | tf_op jit(solution)/shard_map/broadcast_in_dim | solution.py:596

commit v4 on v3

--- a/solution.py
+++ b/solution.py
@@ -77,7 +77,7 @@
         plan += ["U", "n%d" % last, "d%d" % last, "m%d" % (last - 1), "m%d" % last] + every("N")
     plan += [name for name in every("G") if name not in plan]
     plan += ["E"]
-    without = ["d%d" % i for i in DIRECT] + ["m%d" % i for i in groups if i not in RING]
+    without = ["G%d" % (N_GROUPS - 1)] + ["d%d" % i for i in DIRECT] + ["m%d" % i for i in groups if i not in RING]
     return [name for name in plan if name not in without]
 
 
@@ -464,15 +464,16 @@
             each(1, 4, lambda d: normed_spread(i, d).wait_recv())
         relay_copy(i).start()
 
-    def gradient(i):
+    def gradient(i, parts=range(4)):
         m = GROUPS[i][1]
-        relay_copy(i).wait_recv()
-        if i in DIRECT:
-            each(1, 16, lambda j: dpre_copy(i, j).wait_recv())
-        else:
-            each(1, 4, lambda d: dpre_spread(i, d).wait_recv())
+        if 0 in parts:
+            relay_copy(i).wait_recv()
+            if i in DIRECT:
+                each(1, 16, lambda j: dpre_copy(i, j).wait_recv())
+            else:
+                each(1, 4, lambda d: dpre_spread(i, d).wait_recv())
         right = dpa[i][...].reshape(16 * m, block)
-        for c in range(4):
+        for c in parts:
             part = pl.ds(c * 256, 256)
             left = nrm[i][:, :, :, part].reshape(16 * m, 256)
             product = lax.dot_general(left, right, (((0,), (0,)), ((), ())), preferred_element_type=jnp.float32)
@@ -480,6 +481,7 @@
 
     def precondition():
         for i in range(2):
+            gradient(N_GROUPS - 1, (2 * i, 2 * i + 1))
             grad = total[pl.ds(i * block, block), :].astype(jnp.bfloat16)
             lefted = jnp.dot(roots[i, 0], grad, preferred_element_type=jnp.float32).astype(jnp.bfloat16)
             result = jnp.dot(lefted, roots[i, 1], preferred_element_type=jnp.float32).astype(jnp.bfloat16)
@@ -536,7 +538,7 @@
     kinds = dict(F=forward, X=normalise, n=normed_on, m=normed_round, N=relay, B=backward, d=dpre_on, G=gradient)
     for i in range(N_GROUPS):
         for kind, op in kinds.items():
-            if (kind != "d" or i not in DIRECT) and (kind != "m" or i in RING):
+            if (kind != "d" or i not in DIRECT) and (kind != "m" or i in RING) and kind + str(i) != "G%d" % (N_GROUPS - 1):
                 ops[kind + str(i)] = functools.partial(op, i)
     plans = [plan_of(section) for section in range(4)]
 

time: 113 us -> 112 us (level)
  no operation moved by 1% of the time
where the time goes in v4:
time: 112 us
  Pallas kernels  110 us (98%)
  other arithmetic  2.27 us (2%)
    pallas_call x1, Pallas kernels, on_device(): pl.pallas_call(kernel, out_shape=[jax.ShapeDtypeStruct((256, half // 2),...  110 us
    broadcast_in_dim x1, other arithmetic, on_device(): return jnp.concatenate(result, axis=1)[None]  2.27 us

profile of v4, /device:TPU:66, one launch (start us, length us, event | category | flops | bytes accessed | tf_op | source)
XLA Modules:
  0.0 111.9 jit_solution(9414329535197606123)
XLA Ops:
  0.0 109.6 %shard_map.73 = (bf16[256,1024]{1,0:T(8,128)(2,1)}, bf16[256,1024]{1,0:T(8,128)(2,1)}) custom-call(s32[32]{0:T(128)} %bitcast.13, bf16[128,2048]{1,0:T(8,128)(2,1)} %bitcast.11, bf16[4096,2048]{1,0:T(8,128)(2,1)} %bitcast.8, f32[1,4096]{1,0:T(1,128)} %gain.1, bf16[128,2048]{1,0:T(8,128)(2,1)} %bitcast.12, f32[2,512,512]{2,1,0:T(8,128)} %bitcast.9, ...), custom_call_target="tpu_custom_call" | custom-call | tf_op jit(solution)/shard_map/pallas_call | solution.py:585
  109.6 2.3 %maximum_bitcast_fusion = bf16[1,256,2048]{2,1,0:T(8,128)(2,1)} fusion(bf16[256,1024]{1,0:T(8,128)(2,1)} %get-tuple-element.8, bf16[256,1024]{1,0:T(8,128)(2,1)} %get-tuple-element.7), kind=kLoop, calls=%fused_computation | loop fusion | flops 2097152 | bytes 2097152 | tf_op jit(solution)/shard_map/broadcast_in_dim | solution.py:598
